TPU v7x, 32 devices: a whole 2x2x4 slice. The times are simulated.
32 devices in a mesh: row: 4 (over x, core), rhs: 8 (over z, y).
Axes of the slice: x: 2, y: 2, z: 4, core: 2. Of those that a mesh axis runs over, the one named last changes fastest.
Arguments:
- local_rhs: bfloat16 [168, 128, 1024], P('row', None, 'rhs'), may hold values from -6 to 6
- top_rhs: bfloat16 [4, 128, 1024], P('row', None, 'rhs'), may hold values from -6 to 6
- diag_inv: bfloat16 [168, 128, 128], P('row', 'rhs'), as said below
- top_inv: bfloat16 [4, 128, 128], P('row', 'rhs'), as said below
- off_blocks: bfloat16 [168, 4, 128, 128], P('row', None, 'rhs'), may hold values from -0.125 to 0.125
- top_factor: bfloat16 [4, 4, 128, 128], P('row', None, 'rhs'), may hold values from -0.25 to 0.25
- targets: int32 [168, 4], P('row'), may hold values from 24 to 45, as said below
Outputs:
- local_solution: bfloat16 [168, 128, 1024], P('row', None, 'rhs')
- top_solution: bfloat16 [4, 128, 1024], P('row', None, 'rhs')
Inputs may be any that keep to these rules, and one draw needn't show every extreme that they name: `diag_inv`: each block is lower triangular. `top_inv`: each block is lower triangular. `targets`: row r * 42 + k holds 4 distinct codes; a code c < 42 names local supernode r * 42 + c, of a higher level than k; a code c >= 42 names top block c - 42.
All inputs are finite; a program needn't handle non-finite values.
Results may differ from a plain program's by a relative error of at most 0.023.
Values may be sent and summed in bfloat16 or wider, within the bound.
A program may use at most 64 MiB of HBM per device.

v0:
```python
import jax
import jax.numpy as jnp
from jax import lax
from jax.sharding import PartitionSpec as P

LEAF = 24


def spread(shard, axis, root):
    mine = lax.axis_index(axis) == root
    return lax.psum(jnp.where(mine, shard, jnp.zeros_like(shard)), axis)


def local(local_rhs, top_rhs, diag_inv, top_inv, off_blocks, top_factor, targets):
    sub_count = local_rhs.shape[0]
    panel_width = local_rhs.shape[1]
    columns = local_rhs.shape[2]
    top_count = lax.axis_size("row")
    cand_count = sub_count + top_count
    acc_local = jnp.zeros((sub_count, panel_width, columns), jnp.float32)
    acc_top = jnp.zeros((top_count, panel_width, columns), jnp.float32)
    level_ranges = ((0, LEAF), (LEAF, LEAF + LEAF // 2), (LEAF + LEAF // 2, sub_count))
    solved = []
    for first_row, end_row in level_ranges:
        residual_rows = (
            local_rhs[first_row:end_row].astype(jnp.float32) - acc_local[first_row:end_row]
        ).astype(jnp.bfloat16)

        def apply_inverse(slice_part, offset, residual_rows=residual_rows):
            return jnp.einsum(
                "jxm,jme->jxe", slice_part, residual_rows, preferred_element_type=jnp.float32
            )

        level_partial = apply_inverse(
            lax.all_gather(diag_inv[first_row:end_row], "rhs", axis=1, tiled=True), jnp.int32(0)
        ).astype(jnp.bfloat16)
        solved.append(level_partial)
        target_codes = targets[first_row:end_row].reshape(-1)
        later_count = cand_count - end_row
        selector = (
            jnp.arange(later_count, dtype=jnp.int32)[:, None] == target_codes[None, :] - end_row
        ).astype(jnp.float32)

        def spread_updates(slice_part, offset, level_partial=level_partial, selector=selector):
            products = jnp.einsum(
                "yiko,yoq->yikq", slice_part, level_partial, preferred_element_type=jnp.float32
            )
            flattened = products.reshape(selector.shape[1], slice_part.shape[2], columns)
            return jnp.einsum("cn,nar->car", selector, flattened, precision=lax.Precision.HIGHEST)

        contrib = spread_updates(
            lax.all_gather(off_blocks[first_row:end_row], "rhs", axis=2, tiled=True), jnp.int32(0)
        )
        acc_local = acc_local.at[end_row:].add(contrib[: sub_count - end_row])
        acc_top = acc_top + contrib[sub_count - end_row :]
    inverse_rows = top_inv.reshape(1, 1, top_inv.shape[1], panel_width)
    top_full, inv_full = (
        lax.all_gather(top_factor, "rhs", axis=2, tiled=True),
        lax.all_gather(inverse_rows, "rhs", axis=2, tiled=True),
    )
    position = lax.axis_index("row")
    own_sum = lax.psum_scatter(
        acc_top.astype(jnp.bfloat16), "row", scatter_dimension=0, tiled=True
    ).astype(jnp.float32)
    base_value = top_rhs[0].astype(jnp.float32) - own_sum[0]

    def top_step(step_index, carry):
        carried, own_solution = carry
        residual_rows = (base_value - carried).astype(jnp.bfloat16)
        candidate = jnp.dot(
            inv_full[0, 0], residual_rows, preferred_element_type=jnp.float32
        ).astype(jnp.bfloat16)
        solution = spread(candidate, "row", step_index)
        own_solution = jnp.where(position == step_index, solution, own_solution)
        coupling_matrix = lax.dynamic_index_in_dim(top_full[0], step_index, 0, keepdims=False)
        update = jnp.dot(coupling_matrix, solution, preferred_element_type=jnp.float32)
        carried = carried + jnp.where(step_index < position, update, 0.0)
        return (carried, own_solution)

    initial_state = (
        jnp.zeros((panel_width, columns), jnp.float32),
        jnp.zeros((panel_width, columns), jnp.bfloat16),
    )
    own_separator = lax.fori_loop(0, top_count, top_step, initial_state)[1][None]
    return (jnp.concatenate(solved, axis=0), own_separator)


def solution(mesh):
    in_specs = (
        P("row", None, "rhs"),
        P("row", None, "rhs"),
        P("row", "rhs", None),
        P("row", "rhs", None),
        P("row", None, "rhs", None),
        P("row", None, "rhs", None),
        P("row", None),
    )
    out_specs = (P("row", None, "rhs"), P("row", None, "rhs"))
    return jax.shard_map(local, mesh=mesh, in_specs=in_specs, out_specs=out_specs, check_vma=False)
```

profile of v0, /device:TPU:0, one launch (start us, length us, event | category | flops | bytes accessed | tf_op | source)
XLA Modules:
  0.0 296.8 jit_solution(10104199515484747920)
XLA Ops:
  7.2 1.8 slice.103
  9.1 1.6 slice.109
  11.5 35.0 %all_gather.28 = bf16[6,128,128]{2,1,0:T(8,128)(2,1)} all-gather(bf16[6,16,128]{2,1,0:T(8,128)(2,1)S(1)} %slice-done.5), channel_id=1, replica_groups=mesh['row'=4,'rhs'=8] {'rhs'}, dimensions={1}, use_global_device_ids=true | all-gather | bytes 221184 | tf_op jit(solution)/shard_map/all_gather | solution.py:35
  46.5 32.5 %all_gather.26 = bf16[12,128,128]{2,1,0:T(8,128)(2,1)S(1)} all-gather(bf16[12,16,128]{2,1,0:T(8,128)(2,1)S(1)} %slice-done.4), channel_id=1, replica_groups=mesh['row'=4,'rhs'=8] {'rhs'}, dimensions={1}, use_global_device_ids=true | all-gather | bytes 442368 | tf_op jit(solution)/shard_map/all_gather | solution.py:35
  79.0 32.8 %all_gather.24 = bf16[24,128,128]{2,1,0:T(8,128)(2,1)S(1)} all-gather(bf16[24,16,128]{2,1,0:T(8,128)(2,1)S(1)} %slice-done.3), channel_id=1, replica_groups=mesh['row'=4,'rhs'=8] {'rhs'}, dimensions={1}, use_global_device_ids=true | all-gather | bytes 884736 | tf_op jit(solution)/shard_map/all_gather | solution.py:35
  111.8 0.4 convolution_convert_fusion.1
  112.2 35.1 %all_gather.30 = bf16[6,4,128,128]{3,2,1,0:T(8,128)(2,1)} all-gather(bf16[6,4,16,128]{3,2,1,0:T(8,128)(2,1)S(1)} %slice-done.2), channel_id=1, replica_groups=mesh['row'=4,'rhs'=8] {'rhs'}, dimensions={2}, use_global_device_ids=true | all-gather | bytes 884736 | tf_op jit(solution)/shard_map/all_gather | solution.py:52
  147.3 5.6 %fusion.12 = f32[24,128,4,128]{3,1,2,0:T(8,128)} fusion(bf16[24,4,128,128]{3,2,1,0:T(8,128)(2,1)} %all-gather.4.cloned.1.call-done, bf16[24,128,128]{2,1,0:T(8,128)(2,1)S(1)} %convolution_convert_fusion.1), kind=kOutput, calls=%fused_computation.22 | convolution fusion | flops 402653184 | bytes 10223616 | tf_op jit(solution)/shard_map/yiko,yoq->yikq/dot_general | solution.py:45
  152.9 6.6 %copy.46 = f32[96,128,128]{2,0,1:T(8,128)} copy(f32[96,128,128]{1,2,0:T(8,128)} %bitcast.65) | data formatting | bytes 12582912 | tf_op jit(solution)/shard_map/reshape | solution.py:48
  159.5 4.2 %fusion.24 = f32[22,128,128]{2,0,1:T(8,128)S(1)} fusion(f32[96,128,128]{2,0,1:T(8,128)} %copy.46, s32[96]{0:T(128)S(1)} %sub.37), kind=kOutput, calls=%fused_computation.38 | convolution fusion | flops 415238208 | bytes 7733632 | tf_op jit(solution)/shard_map/cn,nar->car/dot_general | solution.py:49
  163.8 1.2 copy-done
  164.9 0.3 fusion.11
  165.2 0.3 convolution_convert_fusion.2
  165.6 3.8 %fusion.17 = f32[12,128,4,128]{3,1,2,0:T(8,128)} fusion(bf16[12,4,128,128]{3,2,1,0:T(8,128)(2,1)} %all-gather.6.cloned.1.call-done, bf16[12,128,128]{1,2,0:T(8,128)(2,1)S(1)} %convolution_convert_fusion.2), kind=kOutput, calls=%fused_computation.28 | convolution fusion | flops 201326592 | bytes 5111808 | tf_op jit(solution)/shard_map/yiko,yoq->yikq/dot_general | solution.py:45
  169.3 2.6 copy.52
  171.9 1.2 fusion.27
  173.2 1.9 fusion.16
  175.1 0.2 convolution_convert_fusion.3
  175.3 1.6 fusion.20
  176.9 2.0 copy.57
  179.0 1.8 fusion.10
  180.8 0.7 copy.58
  181.6 30.4 %all-gather = bf16[1,128,128]{2,1,0:T(8,128)(2,1)S(1)} all-gather(bf16[1,16,128]{2,1,0:T(8,128)(2,1)S(1)} %copy-done.13), channel_id=2, replica_groups=mesh['row'=4,'rhs'=8] {'rhs'}, dimensions={1}, use_global_device_ids=true | all-gather | bytes 36864 | tf_op jit(solution)/shard_map/all_gather | solution.py:59
  212.0 30.5 %all_gather.29 = bf16[1,4,128,128]{3,2,1,0:T(8,128)(2,1)S(1)} all-gather(bf16[1,4,16,128]{3,2,1,0:T(8,128)(2,1)S(1)} %copy-done.12), channel_id=1, replica_groups=mesh['row'=4,'rhs'=8] {'rhs'}, dimensions={2}, use_global_device_ids=true | all-gather | bytes 147456 | tf_op jit(solution)/shard_map/all_gather | solution.py:58
  242.5 2.3 pad_maximum_fusion
  244.8 0.8 subtract_bitcast_fusion
  245.6 44.0 %while.18 = (s32[]{:T(128)}, f32[128,128]{1,0:T(8,128)S(1)}, bf16[128,128]{0,1:T(8,128)(2,1)S(1)}, s32[]{:T(128)}, bf16[1,4,128,128]{3,2,1,0:T(8,128)(2,1)S(1)},...) while((s32[]{:T(128)}, f32[128,128]{1,0:T(8,128)S(1)}, ...), condition=%wide.region_3.4_spmd.clone, body=%wide.region_1.3_spmd.clone.sunk | while | flops 8568841 | bytes 557235 | solution.py:84
  245.8 10.3 %psum.13 = bf16[128,128]{0,1:T(8,128)(2,1)S(1)} all-reduce(bf16[128,128]{0,1:T(8,128)(2,1)S(1)} %fusion.52), channel_id=1, replica_groups=mesh['row'=4,'rhs'=8] {'row'}, use_global_device_ids=true, to_apply=%region_2.2 | all-reduce | flops 16384 | bytes 65536 | tf_op jit(solution)/shard_map/while/body/eval_jaxpr/psum | solution.py:11
  256.5 11.4 %psum.13 = bf16[128,128]{0,1:T(8,128)(2,1)S(1)} all-reduce(bf16[128,128]{0,1:T(8,128)(2,1)S(1)} %fusion.52), channel_id=1, replica_groups=mesh['row'=4,'rhs'=8] {'row'}, use_global_device_ids=true, to_apply=%region_2.2 | all-reduce | flops 16384 | bytes 65536 | tf_op jit(solution)/shard_map/while/body/eval_jaxpr/psum | solution.py:11
  268.4 10.3 %psum.13 = bf16[128,128]{0,1:T(8,128)(2,1)S(1)} all-reduce(bf16[128,128]{0,1:T(8,128)(2,1)S(1)} %fusion.52), channel_id=1, replica_groups=mesh['row'=4,'rhs'=8] {'row'}, use_global_device_ids=true, to_apply=%region_2.2 | all-reduce | flops 16384 | bytes 65536 | tf_op jit(solution)/shard_map/while/body/eval_jaxpr/psum | solution.py:11
  279.1 10.3 %psum.13 = bf16[128,128]{0,1:T(8,128)(2,1)S(1)} all-reduce(bf16[128,128]{0,1:T(8,128)(2,1)S(1)} %fusion.52), channel_id=1, replica_groups=mesh['row'=4,'rhs'=8] {'row'}, use_global_device_ids=true, to_apply=%region_2.2 | all-reduce | flops 16384 | bytes 65536 | tf_op jit(solution)/shard_map/while/body/eval_jaxpr/psum | solution.py:11
  289.6 0.7 copy.59
  (71 shorter events, 2.4 us)
Async XLA Ops:
  7.2 3.6 %copy-start.11 = (s32[42,4]{0,1:T(4,128)S(1)}, s32[42,4]{0,1:T(4,128)}, u32[]{:S(2)}) copy-start(s32[42,4]{0,1:T(4,128)} %param.19) | copy-start | bytes 2020
  7.2 140.2 %all-gather.4.cloned.1.call-start = ((), (), s32[]{:S(2)}) async-start(), calls=%async_computation.1 | async-start | bytes 3538944 | tf_op jit(solution)/shard_map/all_gather | solution.py:52
  9.0 2.5 slice-start.5
  9.0 37.5 %slice-start.4 = ((bf16[42,16,128]{2,1,0:T(8,128)(2,1)}), bf16[12,16,128]{2,1,0:T(8,128)(2,1)S(1)}, s32[]{:S(2)}) async-start(bf16[42,16,128]{2,1,0:T(8,128)(2,1)} %param.15), calls=%async_computation.8 | async-start | bytes 98304 | tf_op jit(solution)/shard_map/slice | solution.py:35
  9.0 70.0 %slice-start.3 = ((bf16[42,16,128]{2,1,0:T(8,128)(2,1)}), bf16[24,16,128]{2,1,0:T(8,128)(2,1)S(1)}, s32[]{:S(2)}) async-start(bf16[42,16,128]{2,1,0:T(8,128)(2,1)} %param.15), calls=%async_computation.7 | async-start | bytes 196608 | tf_op jit(solution)/shard_map/slice | solution.py:35
  9.0 156.5 %all-gather.6.cloned.1.call-start = ((), (), s32[]{:S(2)}) async-start(), calls=%async_computation.2 | async-start | bytes 1769472 | tf_op jit(solution)/shard_map/all_gather | solution.py:52
  10.7 234.1 %reduce-scatter.2.cloned.1.call-start = ((), (), s32[]{:S(2)}) async-start(), calls=%async_computation.3 | async-start | bytes 163840 | tf_op jit(solution)/shard_map/reduce_scatter | solution.py:62
  10.9 100.9 %copy-start.8 = (bf16[42,128,128]{2,1,0:T(8,128)(2,1)S(1)}, bf16[42,128,128]{2,1,0:T(8,128)(2,1)}, u32[]{:S(2)}) copy-start(bf16[42,128,128]{2,1,0:T(8,128)(2,1)} %param.13) | copy-start | bytes 4128772
  79.0 33.2 %slice-start.2 = ((bf16[42,4,16,128]{3,2,1,0:T(8,128)(2,1)}), bf16[6,4,16,128]{3,2,1,0:T(8,128)(2,1)S(1)}, s32[]{:S(2)}) async-start(bf16[42,4,16,128]{3,2,1,0:T(8,128)(2,1)} %param.17), calls=%async_computation.6 | async-start | bytes 196608 | tf_op jit(solution)/shard_map/slice | solution.py:52
  112.2 40.7 %copy-start.1 = (bf16[24,128,128]{2,1,0:T(8,128)(2,1)}, bf16[24,128,128]{2,1,0:T(8,128)(2,1)S(1)}, u32[]{:S(2)}) copy-start(bf16[24,128,128]{2,1,0:T(8,128)(2,1)S(1)} %convolution_convert_fusion.1) | copy-start | bytes 2359300
  159.5 5.4 %slice-start = ((bf16[42,128,128]{2,1,0:T(8,128)(2,1)}), bf16[12,128,128]{2,1,0:T(8,128)(2,1)S(1)}, s32[]{:S(2)}) async-start(bf16[42,128,128]{2,1,0:T(8,128)(2,1)} %param.13), calls=%async_computation.4 | async-start | bytes 786432 | tf_op jit(solution)/shard_map/slice | solution.py:26
  163.8 1.2 copy-start
  165.5 3.8 %copy-start.5 = (bf16[12,128,128]{1,2,0:T(8,128)(2,1)}, bf16[12,128,128]{1,2,0:T(8,128)(2,1)S(1)}, u32[]{:S(2)}) copy-start(bf16[12,128,128]{1,2,0:T(8,128)(2,1)S(1)} %convolution_convert_fusion.2) | copy-start | bytes 1179652
  171.9 1.2 slice-start.1
  173.1 3.8 %copy-start.3 = (f32[10,128,128]{2,0,1:T(8,128)}, f32[10,128,128]{2,0,1:T(8,128)S(1)}, u32[]{:S(2)}) copy-start(f32[10,128,128]{2,0,1:T(8,128)S(1)} %fusion.27) | copy-start | bytes 1966084
  173.1 1.9 copy-start.9
  173.2 2.1 copy-start.6
  175.3 1.6 copy-start.7
  176.9 2.1 copy-start.4
  179.0 2.6 copy-start.13
  179.0 33.0 %copy-start.12 = (bf16[1,4,16,128]{3,2,1,0:T(8,128)(2,1)S(1)}, bf16[1,4,16,128]{3,2,1,0:T(8,128)(2,1)}, u32[]{:S(2)}) copy-start(bf16[1,4,16,128]{3,2,1,0:T(8,128)(2,1)} %param.18) | copy-start | bytes 49156
  179.0 63.5 %copy-start.2 = (bf16[24,128,128]{2,1,0:T(8,128)(2,1)S(1)}, bf16[24,128,128]{2,1,0:T(8,128)(2,1)}, u32[]{:S(2)}) copy-start(bf16[24,128,128]{2,1,0:T(8,128)(2,1)} %copy-done.1) | copy-start | bytes 2359300
  181.5 63.3 %copy-start.10 = (bf16[1,128,128]{2,1,0:T(8,128)(2,1)S(1)}, bf16[1,128,128]{2,1,0:T(8,128)(2,1)}, u32[]{:S(2)}) copy-start(bf16[1,128,128]{2,1,0:T(8,128)(2,1)} %param.14) | copy-start | bytes 98308
Sparse Core Ops, SparseCore 0:
  10.6 74.6 all-gather.3
  87.4 52.3 all-gather.5
  181.7 19.8 reduce-scatter.1
where the time goes:
time: 297 us
  blocking collectives  239 us (80%)
  matrix products  20.4 us (7%)
  local copies, waits for them, and re-layouts  17.8 us (6%)
  between operations  14 us (5%)
  other arithmetic  5.53 us (2%)
    all_gather x3, blocking collectives, local(): lax.all_gather(diag_inv[first_row:end_row], 'rhs', axis=1, tiled=True)  100 us
    psum x4, blocking collectives, spread(): return lax.psum(jnp.where(mine, shard, jnp.zeros_like(shard)), axis)  42.2 us
    all_gather x1, blocking collectives, local(): lax.all_gather(off_blocks[first_row:end_row], 'rhs', axis=2, tiled=True)  35.1 us
    all_gather x1, blocking collectives, local(): lax.all_gather(top_factor, 'rhs', axis=2, tiled=True)  30.5 us
    all_gather x1, blocking collectives, local(): lax.all_gather(inverse_rows, 'rhs', axis=2, tiled=True)  30.4 us
    reshape x3, local copies, waits for them, and re-layouts, spread_updates(): products.reshape(selector.shape[1], slice_part.shape[2], columns)  11.2 us
    dot_general x3, matrix products, spread_updates(): jnp.einsum('yiko,yoq->yikq', slice_part, level_partial, preferred_element...  11 us
    dot_general x3, matrix products, spread_updates(): jnp.einsum('cn,nar->car', selector, flattened, precision=lax.Precision.HI...  7.22 us
  transfers between devices with their start and end apart: 3, of which 0 were waited for; matrix products, arithmetic and copies ran while one was open for 7% of the time, Pallas kernels for 0%

commit v1 on v0

--- a/solution.py
+++ b/solution.py
@@ -1,6 +1,9 @@
+import functools
 import jax
 import jax.numpy as jnp
 from jax import lax
+from jax.experimental import pallas as pl
+from jax.experimental.pallas import tpu as pltpu
 from jax.sharding import PartitionSpec as P
 
 LEAF = 24
@@ -85,6 +88,282 @@
     return (jnp.concatenate(solved, axis=0), own_separator)
 
 
+CHUNK = 3
+LINE = 4
+LEFT, RIGHT, ACROSS = 0, 1, 2
+MESH = pl.DeviceIdType.MESH
+
+
+def detour(k):
+    return lax.rem(k, 6) == 3
+
+
+def relay_kernel(
+    rows, rhs_hbm, top_rhs_hbm, diag_hbm, top_inv_hbm, off_hbm, top_factor_hbm, targets,
+    out_hbm, top_out_hbm,
+    held, held_top, rhs, top_rhs, sol, acc, prod, part, parts, top_sol,
+    load_sem, out_sem, send_sem, recv_sem, row_send, row_recv,
+):
+    sub, width, columns = rhs.shape
+    chunks = 1 + sub // CHUNK
+    cand = sub + rows
+    row, me = lax.axis_index("row"), lax.axis_index("rhs")
+    z, y = me // 2, lax.rem(me, 2)
+    targets_of = {LEFT: me - 2, RIGHT: me + 2, ACROSS: z * 2 + 1 - y}
+    peers = [lax.rem(row + p, rows) for p in range(1, rows)]
+
+    loads = [
+        pltpu.make_async_copy(top_inv_hbm.at[0], held_top.at[row, me, 0], load_sem.at[0]),
+        pltpu.make_async_copy(top_factor_hbm.at[0], held_top.at[row, me, pl.ds(1, 4)], load_sem.at[1]),
+        pltpu.make_async_copy(diag_hbm, held.at[me, :, 0], load_sem.at[2]),
+        pltpu.make_async_copy(off_hbm, held.at[me, :, pl.ds(1, 4)], load_sem.at[3]),
+        pltpu.make_async_copy(top_rhs_hbm.at[0], top_rhs.at[row], load_sem.at[4]),
+        pltpu.make_async_copy(rhs_hbm, rhs, load_sem.at[5]),
+    ]
+    for load in loads:
+        load.start()
+
+    barrier = pltpu.get_barrier_semaphore()
+    for peer in peers:
+        pl.semaphore_signal(barrier, inc=1, device_id=(peer, me), device_id_type=MESH)
+    pl.semaphore_signal(barrier, inc=1, device_id=(row, targets_of[ACROSS]), device_id_type=MESH)
+
+    @pl.when(z > 0)
+    def _():
+        pl.semaphore_signal(barrier, inc=1, device_id=(row, targets_of[LEFT]), device_id_type=MESH)
+
+    @pl.when(z < LINE - 1)
+    def _():
+        pl.semaphore_signal(barrier, inc=1, device_id=(row, targets_of[RIGHT]), device_id_type=MESH)
+
+    def clear(c, carry):
+        acc[c] = jnp.zeros((width, columns), jnp.float32)
+        return carry
+
+    lax.fori_loop(0, cand, clear, 0)
+    for u in range(CHUNK):
+        prod[u * 5 + 4] = jnp.zeros((width, columns), jnp.float32)
+
+    ends = jnp.where(z == 0, 1, 0) + jnp.where(z == LINE - 1, 1, 0)
+    pl.semaphore_wait(barrier, rows + 2 - ends)
+    for load in loads:
+        load.wait()
+
+    def row_copy(kind, p, src, dst):
+        return pltpu.make_async_remote_copy(
+            src_ref=src, dst_ref=dst, send_sem=row_send.at[kind, p], recv_sem=row_recv.at[kind, row],
+            device_id=(peers[p], me), device_id_type=MESH,
+        )
+
+    def row_arrival(kind, p, dst):
+        return pltpu.make_async_remote_copy(
+            src_ref=dst, dst_ref=dst, send_sem=row_send.at[kind, p], recv_sem=row_recv.at[kind, peers[p]],
+            device_id=(peers[p], me), device_id_type=MESH,
+        )
+
+    for p in range(rows - 1):
+        row_copy(0, p, top_rhs.at[row], top_rhs.at[row]).start()
+
+    def either(k, src, count, act):
+        @pl.when(k == 0)
+        def _():
+            act(held_top.at[row, pl.ds(src, count)])
+
+        @pl.when(k > 0)
+        def _():
+            act(held.at[pl.ds(src, count), pl.ds((k - 1) * CHUNK, CHUNK)])
+
+    def describe(ref, k, src, way):
+        return pltpu.make_async_remote_copy(
+            src_ref=ref, dst_ref=ref, send_sem=send_sem.at[way, k], recv_sem=recv_sem.at[k, src],
+            device_id=(row, targets_of[way]), device_id_type=MESH,
+        )
+
+    def relay(k, src, wait, ways):
+        def act(ref):
+            if wait:
+                describe(ref, k, src, ACROSS).wait_recv()
+            for way, wanted in ways:
+                @pl.when(wanted)
+                def _(way=way):
+                    describe(ref, k, src, way).start()
+
+        either(k, src, 1, act)
+
+    def drain(k):
+        around = detour(k)
+        sends = {
+            LEFT: jnp.where(z > 0, (LINE - z) * jnp.where(around, 2, 1), 0),
+            RIGHT: jnp.where(z < LINE - 1, (z + 1) * jnp.where(around, 2, 1), 0),
+            ACROSS: jnp.where(around, 1, LINE),
+        }
+        for way, sizes in ((LEFT, (1, 2, 3, 4, 6)), (RIGHT, (1, 2, 3, 4, 6)), (ACROSS, (1, LINE))):
+            for size in sizes:
+                @pl.when(sends[way] == size)
+                def _(way=way, size=size):
+                    either(k, 0, size, lambda ref: describe(ref, k, 0, way).wait_send())
+
+    def solve(k):
+        first = (k - 1) * CHUNK
+        half = LEAF + LEAF // 2
+        codes = [[targets[first + u, j] for j in range(4)] for u in range(CHUNK)]
+        for u in range(CHUNK):
+            s = first + u
+            residual = (rhs[s].astype(jnp.float32) - acc[s]).astype(jnp.bfloat16)
+            inverse = held[:, s, 0].reshape(width, width)
+            x = jnp.dot(inverse, residual, preferred_element_type=jnp.float32).astype(jnp.bfloat16)
+            sol[s] = x
+            blocks = jnp.concatenate([held[:, s, 1 + j].reshape(width, width) for j in range(4)], axis=0)
+            prod[pl.ds(u * 5, 4)] = jnp.dot(blocks, x, preferred_element_type=jnp.float32).reshape(4, width, columns)
+        pltpu.make_async_copy(sol.at[pl.ds(first, CHUNK)], out_hbm.at[pl.ds(first, CHUNK)], out_sem.at[0]).start()
+
+        def add(c, carry):
+            total = acc[c]
+            for u in range(CHUNK):
+                slot = jnp.int32(u * 5 + 4)
+                for j in range(4):
+                    slot = jnp.where(codes[u][j] == c, u * 5 + j, slot)
+                total = total + prod[slot]
+            acc[c] = total
+            return carry
+
+        lax.fori_loop(jnp.where(first < LEAF, LEAF, jnp.where(first < half, half, sub)), cand, add, 0)
+
+    def step(i, carry):
+        for lag in range(LINE + 1):
+            k = i - lag
+
+            @pl.when((k >= 0) & (k < chunks))
+            def _(k=k, lag=lag):
+                around = detour(k)
+                if lag == 0:
+                    relay(k, me, False, ((LEFT, z > 0), (RIGHT, z < LINE - 1), (ACROSS, z >= 0)))
+                elif lag < LINE:
+                    @pl.when(z >= lag)
+                    def _():
+                        relay(k, me - 2 * lag, True, ((RIGHT, z < LINE - 1), (ACROSS, jnp.logical_not(around))))
+
+                    @pl.when(z + lag < LINE)
+                    def _():
+                        relay(k, me + 2 * lag, True, ((LEFT, z > 0), (ACROSS, jnp.logical_not(around))))
+
+                @pl.when(around)
+                def _():
+                    far, d = targets_of[ACROSS], lag - 1
+                    if d == 0:
+                        relay(k, far, True, ((LEFT, z > 0), (RIGHT, z < LINE - 1)))
+                    elif d > 0:
+                        @pl.when(z >= d)
+                        def _():
+                            relay(k, far - 2 * d, True, ((RIGHT, z < LINE - 1),))
+
+                        @pl.when(z + d < LINE)
+                        def _():
+                            relay(k, far + 2 * d, True, ((LEFT, z > 0),))
+
+        k = i - LINE - 1
+
+        @pl.when(k >= 0)
+        def _():
+            @pl.when(jnp.logical_not(detour(k)))
+            def _():
+                for other in range(LINE):
+                    relay(k, other * 2 + 1 - y, True, ())
+
+            @pl.when(k == 0)
+            def _():
+                for p in range(rows - 1):
+                    row_copy(1, p, held_top.at[row], held_top.at[row]).start()
+
+            @pl.when(k > 0)
+            def _():
+                solve(k)
+
+        @pl.when(i >= 2 * LINE)
+        def _():
+            drain(i - 2 * LINE)
+
+        return carry
+
+    steps = chunks + LINE + 1
+    lax.fori_loop(0, steps, step, 0)
+
+    part[...] = acc[pl.ds(sub, rows)].astype(jnp.bfloat16)
+    for p in range(rows - 1):
+        row_copy(2, p, part, parts.at[row]).start()
+
+    def drain_rest(k, carry):
+        drain(k)
+        return carry
+
+    lax.fori_loop(steps - 2 * LINE, chunks, drain_rest, 0)
+    for p in range(rows - 1):
+        row_copy(0, p, top_rhs.at[row], top_rhs.at[row]).wait_send()
+        row_copy(1, p, held_top.at[row], held_top.at[row]).wait_send()
+        row_arrival(0, p, top_rhs.at[peers[p]]).wait_recv()
+        row_arrival(1, p, held_top.at[peers[p]]).wait_recv()
+    pltpu.make_async_copy(sol, out_hbm, out_sem.at[0]).wait()
+    for p in range(rows - 1):
+        row_arrival(2, p, parts.at[peers[p]]).wait_recv()
+
+    for t in range(rows):
+        base = acc[sub + t]
+        for p in range(rows - 1):
+            base = base + parts[peers[p], t].astype(jnp.float32)
+        base = top_rhs[t].astype(jnp.float32) - base
+        for earlier in range(t):
+            factor = held_top[t, :, 1 + earlier].reshape(width, width)
+            base = base - jnp.dot(factor, top_sol[earlier], preferred_element_type=jnp.float32)
+        inverse = held_top[t, :, 0].reshape(width, width)
+        top_sol[t] = jnp.dot(inverse, base.astype(jnp.bfloat16), preferred_element_type=jnp.float32).astype(jnp.bfloat16)
+    last = pltpu.make_async_copy(top_sol.at[row], top_out_hbm.at[0], out_sem.at[1])
+    last.start()
+    for p in range(rows - 1):
+        row_copy(2, p, part, parts.at[row]).wait_send()
+    last.wait()
+
+
+def relayed(local_rhs, top_rhs, diag_inv, top_inv, off_blocks, top_factor, targets):
+    rows, ranks = lax.axis_size("row"), lax.axis_size("rhs")
+    sub, width, columns = local_rhs.shape
+    share = diag_inv.shape[1]
+    chunks = 1 + sub // CHUNK
+    bf16, f32 = jnp.bfloat16, jnp.float32
+    return pl.pallas_call(
+        functools.partial(relay_kernel, rows),
+        out_shape=(
+            jax.ShapeDtypeStruct(local_rhs.shape, bf16),
+            jax.ShapeDtypeStruct(top_rhs.shape, bf16),
+        ),
+        in_specs=[pl.BlockSpec(memory_space=pl.ANY)] * 6 + [pl.BlockSpec(memory_space=pltpu.SMEM)],
+        out_specs=(pl.BlockSpec(memory_space=pl.ANY),) * 2,
+        scratch_shapes=[
+            pltpu.VMEM((ranks, sub, 5, share, width), bf16),
+            pltpu.VMEM((rows, ranks, 5, share, width), bf16),
+            pltpu.VMEM((sub, width, columns), bf16),
+            pltpu.VMEM((rows, width, columns), bf16),
+            pltpu.VMEM((sub, width, columns), bf16),
+            pltpu.VMEM((sub + rows, width, columns), f32),
+            pltpu.VMEM((5 * CHUNK, width, columns), f32),
+            pltpu.VMEM((rows, width, columns), bf16),
+            pltpu.VMEM((rows, rows, width, columns), bf16),
+            pltpu.VMEM((rows, width, columns), bf16),
+            pltpu.SemaphoreType.DMA((6,)),
+            pltpu.SemaphoreType.DMA((2,)),
+            pltpu.SemaphoreType.DMA((3, chunks)),
+            pltpu.SemaphoreType.DMA((chunks, ranks)),
+            pltpu.SemaphoreType.DMA((3, rows - 1)),
+            pltpu.SemaphoreType.DMA((3, rows)),
+        ],
+        compiler_params=pltpu.CompilerParams(
+            collective_id=0, has_side_effects=True, vmem_limit_bytes=40 * 1024 * 1024
+        ),
+        cost_estimate=pl.CostEstimate(
+            flops=10 * sub * width * width * columns, bytes_accessed=4 * local_rhs.size + 2 * off_blocks.size, transcendentals=0
+        ),
+    )(local_rhs, top_rhs, diag_inv, top_inv, off_blocks, top_factor, targets)
+
+
 def solution(mesh):
     in_specs = (
         P("row", None, "rhs"),
@@ -96,4 +375,5 @@
         P("row", None),
     )
     out_specs = (P("row", None, "rhs"), P("row", None, "rhs"))
-    return jax.shard_map(local, mesh=mesh, in_specs=in_specs, out_specs=out_specs, check_vma=False)
+    body = relayed if mesh.shape["rhs"] == 2 * LINE else local
+    return jax.shard_map(body, mesh=mesh, in_specs=in_specs, out_specs=out_specs, check_vma=False)

time: 297 us -> 94.7 us (0.32)
  blocking collectives: 239 us -> 0 us
  Pallas kernels: 0 us -> 84.9 us
  matrix products: 20.4 us -> 0 us
  between operations: 14 us -> 0.64 us
  local copies, waits for them, and re-layouts: 17.8 us -> 7.99 us
  other arithmetic: 5.53 us -> 0 us
    all_gather x6 -> x0, blocking collectives: 196 us -> none  [the longest x3 100 us: local(): lax.all_gather(diag_inv[first_row:end_row], 'rhs', axis=1, tiled=True)]
    pallas_call x0 -> x1, Pallas kernels: none -> 84.9 us  [relayed(): pl.pallas_call(functools.partial(relay_kernel, rows), out_shape=(jax.Shap...]
    psum x4 -> x0, blocking collectives: 42.2 us -> none  [spread(): return lax.psum(jnp.where(mine, shard, jnp.zeros_like(shard)), axis)]
    dot_general x17 -> x0, matrix products: 20.4 us -> none  [the longest x3 11 us: spread_updates(): jnp.einsum('yiko,yoq->yikq', slice_part, level_partial, preferred_element...]
    reshape x3 -> x0, local copies, waits for them, and re-layouts: 11.2 us -> none  [spread_updates(): products.reshape(selector.shape[1], slice_part.shape[2], columns)]
    unnamed x28 -> x15, local copies, waits for them, and re-layouts: 1.22 us -> 7.99 us
    slice x14 -> x0, local copies, waits for them, and re-layouts: 3.4 us -> none  [the longest x4 3.38 us: local(): off_blocks[first_row:end_row]]
  transfers between devices with their start and end apart: 3 -> 0, of which waited for: 0 -> 0; matrix products, arithmetic and copies ran while one was open for 7% -> 0% of each run, Pallas kernels for 0% -> 0%
where the time goes in v1:
time: 94.7 us; the launch traced here: 93.5 us
  Pallas kernels  84.9 us (90%)
  local copies, waits for them, and re-layouts  7.99 us (8%)
    pallas_call x1, Pallas kernels, relayed(): pl.pallas_call(functools.partial(relay_kernel, rows), out_shape=(jax.Shap...  84.9 us
    unnamed x15, local copies, waits for them, and re-layouts  7.99 us

profile of v1, /device:TPU:0, one launch (start us, length us, event | category | flops | bytes accessed | tf_op | source)
XLA Modules:
  0.0 93.5 jit_solution(12462268686519208760)
XLA Ops:
  0.6 0.8 copy.9.targets
  1.4 0.0 copy-start
  1.4 1.3 %copy-done = bf16[42,128,128]{2,1,0:T(8,128)(2,1)S(1)} copy-done((bf16[42,128,128]{2,1,0:T(8,128)(2,1)S(1)}, bf16[42,128,128]{2,1,0:T(8,128)(2,1)}, u32[]{:S(2)}) %copy-start) | copy-done | bytes 1376280
  2.7 0.0 copy-start.1
  2.8 1.1 %copy-done.1 = bf16[42,4,16,128]{3,2,1,0:T(8,128)(2,1)S(1)} copy-done((bf16[42,4,16,128]{3,2,1,0:T(8,128)(2,1)S(1)}, bf16[42,4,16,128]{3,2,1,0:T(8,128)(2,1)}, u32[]{:S(2)}) %copy-start.1) | copy-done | bytes 688152
  3.8 0.0 copy-start.2
  3.8 0.9 copy-done.2
  4.8 0.0 copy-start.3
  4.8 0.8 copy-done.3
  5.5 0.0 copy-start.4
  5.5 0.7 copy-done.4
  6.2 0.0 copy-start.5
  6.2 0.7 copy-done.5
  6.9 84.9 %shard_map.86 = (bf16[42,128,128]{2,1,0:T(8,128)(2,1)S(1)}, bf16[1,128,128]{2,1,0:T(8,128)(2,1)S(1)}) custom-call(bf16[42,128,128]{2,1,0:T(8,128)(2,1)S(1)} %copy-done, bf16[1,128,128]{2,1,0:T(8,128)(2,1)S(1)} %copy-done.3, bf16[42,16,128]{2,1,0:T(8,128)(2,1)S(1)} %copy-done.2, bf16[1,16,128]{2,1,0:T(8,128)(2,1)S(1)} %copy-done.5, ...), custom_call_target="tpu_custom_call" | custom-call | flops 880803840 | bytes 3440640 | tf_op jit(solution)/shard_map/pallas_call | solution.py:332
  91.8 1.1 %copy.12 = bf16[42,128,128]{2,1,0:T(8,128)(2,1)} copy(bf16[42,128,128]{2,1,0:T(8,128)(2,1)S(1)} %get-tuple-element.4) | data formatting | bytes 2752512
  92.9 0.6 copy.13
Async XLA Ops:
  1.4 1.3 %copy-start = (bf16[42,128,128]{2,1,0:T(8,128)(2,1)S(1)}, bf16[42,128,128]{2,1,0:T(8,128)(2,1)}, u32[]{:S(2)}) copy-start(bf16[42,128,128]{2,1,0:T(8,128)(2,1)} %rhs_hbm.1) | copy-start | bytes 4128772
  2.7 1.1 %copy-start.1 = (bf16[42,4,16,128]{3,2,1,0:T(8,128)(2,1)S(1)}, bf16[42,4,16,128]{3,2,1,0:T(8,128)(2,1)}, u32[]{:S(2)}) copy-start(bf16[42,4,16,128]{3,2,1,0:T(8,128)(2,1)} %off_hbm.1) | copy-start | bytes 2064388
  3.8 0.9 copy-start.2
  4.8 0.8 copy-start.3
  5.5 0.7 copy-start.4
  6.2 0.7 copy-start.5

commit v2 on v1

--- a/solution.py
+++ b/solution.py
@@ -112,16 +112,22 @@
     targets_of = {LEFT: me - 2, RIGHT: me + 2, ACROSS: z * 2 + 1 - y}
     peers = [lax.rem(row + p, rows) for p in range(1, rows)]
 
-    loads = [
-        pltpu.make_async_copy(top_inv_hbm.at[0], held_top.at[row, me, 0], load_sem.at[0]),
-        pltpu.make_async_copy(top_factor_hbm.at[0], held_top.at[row, me, pl.ds(1, 4)], load_sem.at[1]),
-        pltpu.make_async_copy(diag_hbm, held.at[me, :, 0], load_sem.at[2]),
-        pltpu.make_async_copy(off_hbm, held.at[me, :, pl.ds(1, 4)], load_sem.at[3]),
-        pltpu.make_async_copy(top_rhs_hbm.at[0], top_rhs.at[row], load_sem.at[4]),
-        pltpu.make_async_copy(rhs_hbm, rhs, load_sem.at[5]),
+    def load(index, src, dst):
+        return pltpu.make_async_copy(src, dst, load_sem.at[index])
+
+    early, late = pl.ds(0, CHUNK), pl.ds(CHUNK, sub - CHUNK)
+    first_loads = [
+        load(0, top_inv_hbm.at[0], held_top.at[row, me, 0]),
+        load(1, top_factor_hbm.at[0], held_top.at[row, me, pl.ds(1, 4)]),
+        load(2, diag_hbm.at[early], held.at[me, early, 0]),
+        load(3, off_hbm.at[early], held.at[me, early, pl.ds(1, 4)]),
+        load(4, top_rhs_hbm.at[0], top_rhs.at[row]),
     ]
-    for load in loads:
-        load.start()
+    next_loads = [
+        load(5, diag_hbm.at[late], held.at[me, late, 0]),
+        load(6, off_hbm.at[late], held.at[me, late, pl.ds(1, 4)]),
+    ]
+    rhs_load = load(7, rhs_hbm, rhs)
 
     barrier = pltpu.get_barrier_semaphore()
     for peer in peers:
@@ -136,6 +142,9 @@
     def _():
         pl.semaphore_signal(barrier, inc=1, device_id=(row, targets_of[RIGHT]), device_id_type=MESH)
 
+    for copy in first_loads + next_loads + [rhs_load]:
+        copy.start()
+
     def clear(c, carry):
         acc[c] = jnp.zeros((width, columns), jnp.float32)
         return carry
@@ -146,8 +155,8 @@
 
     ends = jnp.where(z == 0, 1, 0) + jnp.where(z == LINE - 1, 1, 0)
     pl.semaphore_wait(barrier, rows + 2 - ends)
-    for load in loads:
-        load.wait()
+    for copy in first_loads:
+        copy.wait()
 
     def row_copy(kind, p, src, dst):
         return pltpu.make_async_remote_copy(
@@ -237,6 +246,11 @@
             def _(k=k, lag=lag):
                 around = detour(k)
                 if lag == 0:
+                    @pl.when(k == 2)
+                    def _():
+                        for copy in next_loads:
+                            copy.wait()
+
                     relay(k, me, False, ((LEFT, z > 0), (RIGHT, z < LINE - 1), (ACROSS, z >= 0)))
                 elif lag < LINE:
                     @pl.when(z >= lag)
@@ -272,6 +286,7 @@
 
             @pl.when(k == 0)
             def _():
+                rhs_load.wait()
                 for p in range(rows - 1):
                     row_copy(1, p, held_top.at[row], held_top.at[row]).start()
 
@@ -348,7 +363,7 @@
             pltpu.VMEM((rows, width, columns), bf16),
             pltpu.VMEM((rows, rows, width, columns), bf16),
             pltpu.VMEM((rows, width, columns), bf16),
-            pltpu.SemaphoreType.DMA((6,)),
+            pltpu.SemaphoreType.DMA((8,)),
             pltpu.SemaphoreType.DMA((2,)),
             pltpu.SemaphoreType.DMA((3, chunks)),
             pltpu.SemaphoreType.DMA((chunks, ranks)),
@@ -356,7 +371,7 @@
             pltpu.SemaphoreType.DMA((3, rows)),
         ],
         compiler_params=pltpu.CompilerParams(
-            collective_id=0, has_side_effects=True, vmem_limit_bytes=40 * 1024 * 1024
+            collective_id=0, has_side_effects=True, vmem_limit_bytes=60 * 1024 * 1024
         ),
         cost_estimate=pl.CostEstimate(
             flops=10 * sub * width * width * columns, bytes_accessed=4 * local_rhs.size + 2 * off_blocks.size, transcendentals=0

time: 94.7 us -> 91.2 us (0.963)
  local copies, waits for them, and re-layouts: 7.99 us -> 4.57 us
    unnamed x15 -> x5, local copies, waits for them, and re-layouts: 7.99 us -> 4.57 us
where the time goes in v2:
time: 91.2 us; the launch traced here: 90.1 us
  Pallas kernels  84.9 us (93%)
  local copies, waits for them, and re-layouts  4.57 us (5%)
    pallas_call x1, Pallas kernels, relayed(): pl.pallas_call(functools.partial(relay_kernel, rows), out_shape=(jax.Shap...  84.9 us
    unnamed x5, local copies, waits for them, and re-layouts  4.57 us

profile of v2, /device:TPU:0, one launch (start us, length us, event | category | flops | bytes accessed | tf_op | source)
XLA Modules:
  0.0 90.1 jit_solution(16185349048735529818)
XLA Ops:
  0.6 1.4 %copy.9.targets = s32[42,4]{1,0:T(8,128)} copy(s32[42,4]{0,1:T(4,128)} %param.13) | data formatting | bytes 1344 | tf_op args[6]
  2.0 84.9 %shard_map.86 = (bf16[42,128,128]{2,1,0:T(8,128)(2,1)}, bf16[1,128,128]{2,1,0:T(8,128)(2,1)}) custom-call(bf16[42,128,128]{2,1,0:T(8,128)(2,1)} %rhs_hbm.1, bf16[1,128,128]{2,1,0:T(8,128)(2,1)} %top_rhs_hbm.1, bf16[42,16,128]{2,1,0:T(8,128)(2,1)} %diag_hbm.1, bf16[1,16,128]{2,1,0:T(8,128)(2,1)} %top_inv_hbm.1, bf16[42,4,16,128]{3,2,1,0:T(8,128)(2,1)} %off_hbm.1, ...), custom_call_target="tpu_custom_call" | custom-call | flops 880803840 | bytes 3440640 | tf_op jit(solution)/shard_map/pallas_call | solution.py:347
  86.9 0.0 copy-start
  86.9 2.6 %copy.12 = bf16[42,128,128]{2,1,0:T(8,128)(2,1)} copy(bf16[42,128,128]{2,1,0:T(8,128)(2,1)} %get-tuple-element.4) | data formatting | bytes 2752512
  89.5 0.0 copy-done
  89.5 0.6 copy.13
Async XLA Ops:
  86.9 2.6 %copy-start = (bf16[1,128,128]{2,1,0:T(8,128)(2,1)S(1)}, bf16[1,128,128]{2,1,0:T(8,128)(2,1)}, u32[]{:S(2)}) copy-start(bf16[1,128,128]{2,1,0:T(8,128)(2,1)} %get-tuple-element.5) | copy-start | bytes 98308

commit v3 on v2

--- a/solution.py
+++ b/solution.py
@@ -88,8 +88,10 @@
     return (jnp.concatenate(solved, axis=0), own_separator)
 
 
-CHUNK = 3
+CHUNK = 2
 LINE = 4
+HOP = 2
+READY = HOP * (LINE - 1) + 1
 LEFT, RIGHT, ACROSS = 0, 1, 2
 MESH = pl.DeviceIdType.MESH
 
@@ -239,43 +241,45 @@
         lax.fori_loop(jnp.where(first < LEAF, LEAF, jnp.where(first < half, half, sub)), cand, add, 0)
 
     def step(i, carry):
-        for lag in range(LINE + 1):
-            k = i - lag
+        for d in range(LINE):
+            k = i - HOP * d
 
             @pl.when((k >= 0) & (k < chunks))
-            def _(k=k, lag=lag):
-                around = detour(k)
-                if lag == 0:
+            def _(k=k, d=d):
+                straight = jnp.logical_not(detour(k))
+                if d == 0:
                     @pl.when(k == 2)
                     def _():
                         for copy in next_loads:
                             copy.wait()
 
                     relay(k, me, False, ((LEFT, z > 0), (RIGHT, z < LINE - 1), (ACROSS, z >= 0)))
-                elif lag < LINE:
-                    @pl.when(z >= lag)
-                    def _():
-                        relay(k, me - 2 * lag, True, ((RIGHT, z < LINE - 1), (ACROSS, jnp.logical_not(around))))
-
-                    @pl.when(z + lag < LINE)
-                    def _():
-                        relay(k, me + 2 * lag, True, ((LEFT, z > 0), (ACROSS, jnp.logical_not(around))))
-
-                @pl.when(around)
-                def _():
-                    far, d = targets_of[ACROSS], lag - 1
-                    if d == 0:
-                        relay(k, far, True, ((LEFT, z > 0), (RIGHT, z < LINE - 1)))
-                    elif d > 0:
-                        @pl.when(z >= d)
-                        def _():
-                            relay(k, far - 2 * d, True, ((RIGHT, z < LINE - 1),))
-
-                        @pl.when(z + d < LINE)
-                        def _():
-                            relay(k, far + 2 * d, True, ((LEFT, z > 0),))
-
-        k = i - LINE - 1
+                else:
+                    @pl.when(z >= d)
+                    def _():
+                        relay(k, me - 2 * d, True, ((RIGHT, z < LINE - 1), (ACROSS, straight)))
+
+                    @pl.when(z + d < LINE)
+                    def _():
+                        relay(k, me + 2 * d, True, ((LEFT, z > 0), (ACROSS, straight)))
+
+            k = i - HOP * d - 1
+
+            @pl.when((k >= 0) & (k < chunks) & detour(k))
+            def _(k=k, d=d):
+                far = targets_of[ACROSS]
+                if d == 0:
+                    relay(k, far, True, ((LEFT, z > 0), (RIGHT, z < LINE - 1)))
+                else:
+                    @pl.when(z >= d)
+                    def _():
+                        relay(k, far - 2 * d, True, ((RIGHT, z < LINE - 1),))
+
+                    @pl.when(z + d < LINE)
+                    def _():
+                        relay(k, far + 2 * d, True, ((LEFT, z > 0),))
+
+        k = i - READY
 
         @pl.when(k >= 0)
         def _():
@@ -294,13 +298,13 @@
             def _():
                 solve(k)
 
-        @pl.when(i >= 2 * LINE)
+        @pl.when(i > READY)
         def _():
-            drain(i - 2 * LINE)
+            drain(i - READY - 1)
 
         return carry
 
-    steps = chunks + LINE + 1
+    steps = chunks + READY
     lax.fori_loop(0, steps, step, 0)
 
     part[...] = acc[pl.ds(sub, rows)].astype(jnp.bfloat16)
@@ -311,7 +315,7 @@
         drain(k)
         return carry
 
-    lax.fori_loop(steps - 2 * LINE, chunks, drain_rest, 0)
+    lax.fori_loop(chunks - 1, chunks, drain_rest, 0)
     for p in range(rows - 1):
         row_copy(0, p, top_rhs.at[row], top_rhs.at[row]).wait_send()
         row_copy(1, p, held_top.at[row], held_top.at[row]).wait_send()
@@ -350,7 +354,7 @@
             jax.ShapeDtypeStruct(local_rhs.shape, bf16),
             jax.ShapeDtypeStruct(top_rhs.shape, bf16),
         ),
-        in_specs=[pl.BlockSpec(memory_space=pl.ANY)] * 6 + [pl.BlockSpec(memory_space=pltpu.SMEM)],
+        in_specs=[pl.BlockSpec(memory_space=pltpu.HBM)] * 6 + [pl.BlockSpec(memory_space=pltpu.SMEM)],
         out_specs=(pl.BlockSpec(memory_space=pl.ANY),) * 2,
         scratch_shapes=[
             pltpu.VMEM((ranks, sub, 5, share, width), bf16),

time: 91.2 us -> 94.4 us (1.035)
  Pallas kernels: 84.9 us -> 88.1 us
    pallas_call x1, Pallas kernels: 84.9 us -> 88.1 us  [relayed(): pl.pallas_call(functools.partial(relay_kernel, rows), out_shape=(jax.Shap...]
where the time goes in v3:
time: 94.4 us; the launch traced here: 93.3 us
  Pallas kernels  88.1 us (93%)
  local copies, waits for them, and re-layouts  4.57 us (5%)
    pallas_call x1, Pallas kernels, relayed(): pl.pallas_call(functools.partial(relay_kernel, rows), out_shape=(jax.Shap...  88.1 us
    unnamed x5, local copies, waits for them, and re-layouts  4.57 us

profile of v3, /device:TPU:0, one launch (start us, length us, event | category | flops | bytes accessed | tf_op | source)
XLA Modules:
  0.0 93.3 jit_solution(12249796847610293434)
XLA Ops:
  0.6 1.4 %copy.9.targets = s32[42,4]{1,0:T(8,128)} copy(s32[42,4]{0,1:T(4,128)} %param.13) | data formatting | bytes 1344 | tf_op args[6]
  2.0 88.1 %shard_map.86 = (bf16[42,128,128]{2,1,0:T(8,128)(2,1)}, bf16[1,128,128]{2,1,0:T(8,128)(2,1)}) custom-call(bf16[42,128,128]{2,1,0:T(8,128)(2,1)} %rhs_hbm.1, bf16[1,128,128]{2,1,0:T(8,128)(2,1)} %top_rhs_hbm.1, bf16[42,16,128]{2,1,0:T(8,128)(2,1)} %diag_hbm.1, bf16[1,16,128]{2,1,0:T(8,128)(2,1)} %top_inv_hbm.1, bf16[42,4,16,128]{3,2,1,0:T(8,128)(2,1)} %off_hbm.1, ...), custom_call_target="tpu_custom_call" | custom-call | flops 880803840 | bytes 3440640 | tf_op jit(solution)/shard_map/pallas_call | solution.py:351
  90.1 0.0 copy-start
  90.2 2.6 %copy.12 = bf16[42,128,128]{2,1,0:T(8,128)(2,1)} copy(bf16[42,128,128]{2,1,0:T(8,128)(2,1)} %get-tuple-element.4) | data formatting | bytes 2752512
  92.7 0.0 copy-done
  92.7 0.6 copy.13
Async XLA Ops:
  90.1 2.6 %copy-start = (bf16[1,128,128]{2,1,0:T(8,128)(2,1)S(1)}, bf16[1,128,128]{2,1,0:T(8,128)(2,1)}, u32[]{:S(2)}) copy-start(bf16[1,128,128]{2,1,0:T(8,128)(2,1)} %get-tuple-element.5) | copy-start | bytes 98308

commit v4 on v3

--- a/solution.py
+++ b/solution.py
@@ -88,16 +88,16 @@
     return (jnp.concatenate(solved, axis=0), own_separator)
 
 
-CHUNK = 2
+CHUNK = 3
 LINE = 4
-HOP = 2
+HOP = 1
 READY = HOP * (LINE - 1) + 1
 LEFT, RIGHT, ACROSS = 0, 1, 2
 MESH = pl.DeviceIdType.MESH
 
 
 def detour(k):
-    return lax.rem(k, 6) == 3
+    return k == 7
 
 
 def relay_kernel(
@@ -217,28 +217,37 @@
     def solve(k):
         first = (k - 1) * CHUNK
         half = LEAF + LEAF // 2
-        codes = [[targets[first + u, j] for j in range(4)] for u in range(CHUNK)]
+        codes = [[targets[j, first + u] for j in range(4)] for u in range(CHUNK)]
+        residuals = [
+            (rhs[first + u].astype(jnp.float32) - acc[first + u]).astype(jnp.bfloat16) for u in range(CHUNK)
+        ]
+        solved = [
+            jnp.dot(held[:, first + u, 0].reshape(width, width), residuals[u], preferred_element_type=jnp.float32)
+            for u in range(CHUNK)
+        ]
+        solved = [x.astype(jnp.bfloat16) for x in solved]
         for u in range(CHUNK):
-            s = first + u
-            residual = (rhs[s].astype(jnp.float32) - acc[s]).astype(jnp.bfloat16)
-            inverse = held[:, s, 0].reshape(width, width)
-            x = jnp.dot(inverse, residual, preferred_element_type=jnp.float32).astype(jnp.bfloat16)
-            sol[s] = x
-            blocks = jnp.concatenate([held[:, s, 1 + j].reshape(width, width) for j in range(4)], axis=0)
-            prod[pl.ds(u * 5, 4)] = jnp.dot(blocks, x, preferred_element_type=jnp.float32).reshape(4, width, columns)
+            sol[first + u] = solved[u]
+        for u in range(CHUNK):
+            blocks = [held[:, first + u, 1 + j].reshape(width, width) for j in range(4)]
+            updates = jnp.dot(jnp.concatenate(blocks, axis=0), solved[u], preferred_element_type=jnp.float32)
+            prod[pl.ds(u * 5, 4)] = updates.reshape(4, width, columns)
         pltpu.make_async_copy(sol.at[pl.ds(first, CHUNK)], out_hbm.at[pl.ds(first, CHUNK)], out_sem.at[0]).start()
 
-        def add(c, carry):
-            total = acc[c]
-            for u in range(CHUNK):
-                slot = jnp.int32(u * 5 + 4)
-                for j in range(4):
-                    slot = jnp.where(codes[u][j] == c, u * 5 + j, slot)
-                total = total + prod[slot]
-            acc[c] = total
+        least = jnp.where(first < LEAF, LEAF, jnp.where(first < half, half, sub))
+
+        def add(pair, carry):
+            for c in (least + 2 * pair, least + 2 * pair + 1):
+                total = acc[c]
+                for u in range(CHUNK):
+                    slot = jnp.int32(u * 5 + 4)
+                    for j in range(4):
+                        slot = jnp.where(codes[u][j] == c, u * 5 + j, slot)
+                    total = total + prod[slot]
+                acc[c] = total
             return carry
 
-        lax.fori_loop(jnp.where(first < LEAF, LEAF, jnp.where(first < half, half, sub)), cand, add, 0)
+        lax.fori_loop(0, (cand - least) // 2, add, 0)
 
     def step(i, carry):
         for d in range(LINE):
@@ -342,13 +351,38 @@
     last.wait()
 
 
+def place_kernel(local_in, top_in, local_out, top_out, sems):
+    sub = local_in.shape[0]
+    parts = [pl.ds(first, CHUNK) for first in range(0, sub, CHUNK)]
+    copies = [
+        pltpu.make_async_copy(local_in.at[part], local_out.at[part], sems.at[1 + index])
+        for index, part in enumerate(parts)
+    ]
+    copies.append(pltpu.make_async_copy(top_in, top_out, sems.at[0]))
+    for copy in copies:
+        copy.start()
+    for copy in copies:
+        copy.wait()
+
+
+def placed(local_solution, top_solution):
+    pieces = local_solution.shape[0] // CHUNK
+    return pl.pallas_call(
+        place_kernel,
+        out_shape=tuple(jax.ShapeDtypeStruct(x.shape, x.dtype) for x in (local_solution, top_solution)),
+        in_specs=[pl.BlockSpec(memory_space=pl.ANY)] * 2,
+        out_specs=(pl.BlockSpec(memory_space=pl.ANY),) * 2,
+        scratch_shapes=[pltpu.SemaphoreType.DMA((1 + pieces,))],
+    )(local_solution, top_solution)
+
+
 def relayed(local_rhs, top_rhs, diag_inv, top_inv, off_blocks, top_factor, targets):
     rows, ranks = lax.axis_size("row"), lax.axis_size("rhs")
     sub, width, columns = local_rhs.shape
     share = diag_inv.shape[1]
     chunks = 1 + sub // CHUNK
     bf16, f32 = jnp.bfloat16, jnp.float32
-    return pl.pallas_call(
+    solutions = pl.pallas_call(
         functools.partial(relay_kernel, rows),
         out_shape=(
             jax.ShapeDtypeStruct(local_rhs.shape, bf16),
@@ -380,7 +414,8 @@
         cost_estimate=pl.CostEstimate(
             flops=10 * sub * width * width * columns, bytes_accessed=4 * local_rhs.size + 2 * off_blocks.size, transcendentals=0
         ),
-    )(local_rhs, top_rhs, diag_inv, top_inv, off_blocks, top_factor, targets)
+    )(local_rhs, top_rhs, diag_inv, top_inv, off_blocks, top_factor, targets.T)
+    return placed(*solutions)
 
 
 def solution(mesh):

time: 94.4 us -> 134 us (1.42)
  Pallas kernels: 88.1 us -> 132 us
  local copies, waits for them, and re-layouts: 4.57 us -> 0 us
    pallas_call x0 -> x1, Pallas kernels: none -> 43.9 us  [placed(): pl.pallas_call(place_kernel, out_shape=tuple((jax.ShapeDtypeStruct(x.shap...]
    unnamed x5 -> x0, local copies, waits for them, and re-layouts: 4.57 us -> none
where the time goes in v4:
time: 134 us; the launch traced here: 133 us
  Pallas kernels  132 us (99%)
    pallas_call x1, Pallas kernels, relayed(): pl.pallas_call(functools.partial(relay_kernel, rows), out_shape=(jax.Shap...  88.4 us
    pallas_call x1, Pallas kernels, placed(): pl.pallas_call(place_kernel, out_shape=tuple((jax.ShapeDtypeStruct(x.shap...  43.9 us

profile of v4, /device:TPU:0, one launch (start us, length us, event | category | flops | bytes accessed | tf_op | source)
XLA Modules:
  0.0 133.0 jit_solution(5869427761509413725)
XLA Ops:
  0.6 88.4 %shard_map.86 = (bf16[42,128,128]{2,1,0:T(8,128)(2,1)}, bf16[1,128,128]{2,1,0:T(8,128)(2,1)}) custom-call(bf16[42,128,128]{2,1,0:T(8,128)(2,1)} %rhs_hbm.1, bf16[1,128,128]{2,1,0:T(8,128)(2,1)} %top_rhs_hbm.1, bf16[42,16,128]{2,1,0:T(8,128)(2,1)} %diag_hbm.1, bf16[1,16,128]{2,1,0:T(8,128)(2,1)} %top_inv_hbm.1, bf16[42,4,16,128]{3,2,1,0:T(8,128)(2,1)} %off_hbm.1, ...), custom_call_target="tpu_custom_call" | custom-call | flops 880803840 | bytes 3440640 | tf_op jit(solution)/shard_map/pallas_call | solution.py:385
  89.1 43.9 %shard_map.87 = (bf16[42,128,128]{2,1,0:T(8,128)(2,1)}, bf16[1,128,128]{2,1,0:T(8,128)(2,1)}) custom-call(bf16[42,128,128]{2,1,0:T(8,128)(2,1)} %get-tuple-element.4.local_in, bf16[1,128,128]{2,1,0:T(8,128)(2,1)} %get-tuple-element.5.top_in), custom_call_target="tpu_custom_call" | custom-call | tf_op jit(solution)/shard_map/pallas_call | solution.py:370

commit v5 on v4

--- a/solution.py
+++ b/solution.py
@@ -88,27 +88,33 @@
     return (jnp.concatenate(solved, axis=0), own_separator)
 
 
-CHUNK = 3
+CHUNK = 2
 LINE = 4
-HOP = 1
+HOP = 2
 READY = HOP * (LINE - 1) + 1
 LEFT, RIGHT, ACROSS = 0, 1, 2
 MESH = pl.DeviceIdType.MESH
 
 
 def detour(k):
-    return k == 7
+    return lax.rem(k, 6) == 3
+
+
+def times_turned(left, right):
+    return lax.dot_general(left, right, (((1,), (1,)), ((), ())), preferred_element_type=jnp.float32)
 
 
 def relay_kernel(
     rows, rhs_hbm, top_rhs_hbm, diag_hbm, top_inv_hbm, off_hbm, top_factor_hbm, targets,
     out_hbm, top_out_hbm,
     held, held_top, rhs, top_rhs, sol, acc, prod, part, parts, top_sol,
-    load_sem, out_sem, send_sem, recv_sem, row_send, row_recv,
+    turned, top_rhs_turned, gathered, top_out,
+    load_sem, out_sem, send_sem, recv_sem, row_send, row_recv, top_send, top_recv,
 ):
     sub, width, columns = rhs.shape
     chunks = 1 + sub // CHUNK
     cand = sub + rows
+    share = columns // rows
     row, me = lax.axis_index("row"), lax.axis_index("rhs")
     z, y = me // 2, lax.rem(me, 2)
     targets_of = {LEFT: me - 2, RIGHT: me + 2, ACROSS: z * 2 + 1 - y}
@@ -301,6 +307,10 @@
             def _():
                 rhs_load.wait()
                 for p in range(rows - 1):
+                    row_arrival(0, p, top_rhs.at[peers[p]]).wait_recv()
+                for t in range(rows):
+                    top_rhs_turned[t] = top_rhs[t].astype(jnp.float32).T
+                for p in range(rows - 1):
                     row_copy(1, p, held_top.at[row], held_top.at[row]).start()
 
             @pl.when(k > 0)
@@ -316,9 +326,13 @@
     steps = chunks + READY
     lax.fori_loop(0, steps, step, 0)
 
-    part[...] = acc[pl.ds(sub, rows)].astype(jnp.bfloat16)
-    for p in range(rows - 1):
-        row_copy(2, p, part, parts.at[row]).start()
+    mine = pl.ds(pl.multiple_of(row * share, share), share)
+    for t in range(rows):
+        turned[t] = acc[sub + t].T
+        part[t] = turned[t].astype(jnp.bfloat16)
+    slices = [part.at[:, pl.ds(pl.multiple_of(peer * share, share), share)] for peer in peers]
+    for p in range(rows - 1):
+        row_copy(2, p, slices[p], parts.at[row]).start()
 
     def drain_rest(k, carry):
         drain(k)
@@ -328,37 +342,59 @@
     for p in range(rows - 1):
         row_copy(0, p, top_rhs.at[row], top_rhs.at[row]).wait_send()
         row_copy(1, p, held_top.at[row], held_top.at[row]).wait_send()
-        row_arrival(0, p, top_rhs.at[peers[p]]).wait_recv()
         row_arrival(1, p, held_top.at[peers[p]]).wait_recv()
     pltpu.make_async_copy(sol, out_hbm, out_sem.at[0]).wait()
     for p in range(rows - 1):
         row_arrival(2, p, parts.at[peers[p]]).wait_recv()
 
+    def solved_copy(t):
+        return pltpu.make_async_remote_copy(
+            src_ref=top_sol.at[t], dst_ref=gathered.at[row], send_sem=top_send.at[t], recv_sem=top_recv.at[row],
+            device_id=(t, me), device_id_type=MESH,
+        )
+
     for t in range(rows):
-        base = acc[sub + t]
+        base = turned[t, mine]
         for p in range(rows - 1):
             base = base + parts[peers[p], t].astype(jnp.float32)
-        base = top_rhs[t].astype(jnp.float32) - base
+        base = top_rhs_turned[t, mine] - base
         for earlier in range(t):
             factor = held_top[t, :, 1 + earlier].reshape(width, width)
-            base = base - jnp.dot(factor, top_sol[earlier], preferred_element_type=jnp.float32)
+            base = base - times_turned(top_sol[earlier], factor)
         inverse = held_top[t, :, 0].reshape(width, width)
-        top_sol[t] = jnp.dot(inverse, base.astype(jnp.bfloat16), preferred_element_type=jnp.float32).astype(jnp.bfloat16)
-    last = pltpu.make_async_copy(top_sol.at[row], top_out_hbm.at[0], out_sem.at[1])
+        top_sol[t] = times_turned(base.astype(jnp.bfloat16), inverse).astype(jnp.bfloat16)
+
+        @pl.when(row != t)
+        def _(t=t):
+            solved_copy(t).start()
+
+        @pl.when(row == t)
+        def _(t=t):
+            gathered[row] = top_sol[t]
+
+    for p in range(rows - 1):
+        pltpu.make_async_remote_copy(
+            src_ref=top_sol.at[0], dst_ref=gathered.at[peers[p]], send_sem=top_send.at[0], recv_sem=top_recv.at[peers[p]],
+            device_id=(peers[p], me), device_id_type=MESH,
+        ).wait_recv()
+    owned = gathered[...].reshape(columns, width).astype(jnp.float32)
+    top_out[...] = owned.T.astype(jnp.bfloat16)
+    last = pltpu.make_async_copy(top_out, top_out_hbm.at[0], out_sem.at[1])
     last.start()
     for p in range(rows - 1):
-        row_copy(2, p, part, parts.at[row]).wait_send()
+        row_copy(2, p, slices[p], parts.at[row]).wait_send()
+    for t in range(rows):
+        @pl.when(row != t)
+        def _(t=t):
+            solved_copy(t).wait_send()
     last.wait()
 
 
 def place_kernel(local_in, top_in, local_out, top_out, sems):
-    sub = local_in.shape[0]
-    parts = [pl.ds(first, CHUNK) for first in range(0, sub, CHUNK)]
     copies = [
-        pltpu.make_async_copy(local_in.at[part], local_out.at[part], sems.at[1 + index])
-        for index, part in enumerate(parts)
+        pltpu.make_async_copy(local_in, local_out, sems.at[0]),
+        pltpu.make_async_copy(top_in, top_out, sems.at[1]),
     ]
-    copies.append(pltpu.make_async_copy(top_in, top_out, sems.at[0]))
     for copy in copies:
         copy.start()
     for copy in copies:
@@ -366,13 +402,13 @@
 
 
 def placed(local_solution, top_solution):
-    pieces = local_solution.shape[0] // CHUNK
     return pl.pallas_call(
         place_kernel,
         out_shape=tuple(jax.ShapeDtypeStruct(x.shape, x.dtype) for x in (local_solution, top_solution)),
-        in_specs=[pl.BlockSpec(memory_space=pl.ANY)] * 2,
+        in_specs=[pl.BlockSpec(memory_space=pltpu.VMEM)] * 2,
         out_specs=(pl.BlockSpec(memory_space=pl.ANY),) * 2,
-        scratch_shapes=[pltpu.SemaphoreType.DMA((1 + pieces,))],
+        scratch_shapes=[pltpu.SemaphoreType.DMA((2,))],
+        compiler_params=pltpu.CompilerParams(vmem_limit_bytes=32 * 1024 * 1024),
     )(local_solution, top_solution)
 
 
@@ -399,14 +435,20 @@
             pltpu.VMEM((sub + rows, width, columns), f32),
             pltpu.VMEM((5 * CHUNK, width, columns), f32),
             pltpu.VMEM((rows, width, columns), bf16),
-            pltpu.VMEM((rows, rows, width, columns), bf16),
-            pltpu.VMEM((rows, width, columns), bf16),
+            pltpu.VMEM((rows, rows, columns // rows, width), bf16),
+            pltpu.VMEM((rows, columns // rows, width), bf16),
+            pltpu.VMEM((rows, columns, width), f32),
+            pltpu.VMEM((rows, columns, width), f32),
+            pltpu.VMEM((rows, columns // rows, width), bf16),
+            pltpu.VMEM((width, columns), bf16),
             pltpu.SemaphoreType.DMA((8,)),
             pltpu.SemaphoreType.DMA((2,)),
             pltpu.SemaphoreType.DMA((3, chunks)),
             pltpu.SemaphoreType.DMA((chunks, ranks)),
             pltpu.SemaphoreType.DMA((3, rows - 1)),
             pltpu.SemaphoreType.DMA((3, rows)),
+            pltpu.SemaphoreType.DMA((rows,)),
+            pltpu.SemaphoreType.DMA((rows,)),
         ],
         compiler_params=pltpu.CompilerParams(
             collective_id=0, has_side_effects=True, vmem_limit_bytes=60 * 1024 * 1024

time: 134 us -> 92.3 us (0.69)
  Pallas kernels: 132 us -> 89.3 us
  local copies, waits for them, and re-layouts: 0 us -> 2.09 us
    pallas_call x1, Pallas kernels: 43.9 us -> 1.1 us  [placed(): pl.pallas_call(place_kernel, out_shape=tuple((jax.ShapeDtypeStruct(x.shap...]
    unnamed x0 -> x4, local copies, waits for them, and re-layouts: none -> 2.09 us
where the time goes in v5:
time: 92.3 us; the launch traced here: 92 us
  Pallas kernels  89.3 us (97%)
  local copies, waits for them, and re-layouts  2.09 us (2%)
    pallas_call x1, Pallas kernels, relayed(): pl.pallas_call(functools.partial(relay_kernel, rows), out_shape=(jax.Shap...  88.2 us
    unnamed x4, local copies, waits for them, and re-layouts  2.09 us

profile of v5, /device:TPU:0, one launch (start us, length us, event | category | flops | bytes accessed | tf_op | source)
XLA Modules:
  0.0 92.0 jit_solution(16438068158403273823)
XLA Ops:
  0.6 88.2 %shard_map.86 = (bf16[42,128,128]{2,1,0:T(8,128)(2,1)}, bf16[1,128,128]{2,1,0:T(8,128)(2,1)}) custom-call(bf16[42,128,128]{2,1,0:T(8,128)(2,1)} %rhs_hbm.1, bf16[1,128,128]{2,1,0:T(8,128)(2,1)} %top_rhs_hbm.1, bf16[42,16,128]{2,1,0:T(8,128)(2,1)} %diag_hbm.1, bf16[1,16,128]{2,1,0:T(8,128)(2,1)} %top_inv_hbm.1, bf16[42,4,16,128]{3,2,1,0:T(8,128)(2,1)} %off_hbm.1, ...), custom_call_target="tpu_custom_call" | custom-call | flops 880803840 | bytes 3440640 | tf_op jit(solution)/shard_map/pallas_call | solution.py:421
  88.8 0.0 copy-start
  88.8 1.3 %copy-done = bf16[42,128,128]{2,1,0:T(8,128)(2,1)S(1)} copy-done((bf16[42,128,128]{2,1,0:T(8,128)(2,1)S(1)}, bf16[42,128,128]{2,1,0:T(8,128)(2,1)}, u32[]{:S(2)}) %copy-start) | copy-done | bytes 1376280
  90.2 0.0 copy-start.1
  90.2 0.8 copy-done.1
  90.9 1.1 %shard_map.87 = (bf16[42,128,128]{2,1,0:T(8,128)(2,1)}, bf16[1,128,128]{2,1,0:T(8,128)(2,1)}) custom-call(bf16[42,128,128]{2,1,0:T(8,128)(2,1)S(1)} %copy-done, bf16[1,128,128]{2,1,0:T(8,128)(2,1)S(1)} %copy-done.1), custom_call_target="tpu_custom_call" | custom-call | tf_op jit(solution)/shard_map/pallas_call | solution.py:405
Async XLA Ops:
  88.8 1.3 %copy-start = (bf16[42,128,128]{2,1,0:T(8,128)(2,1)S(1)}, bf16[42,128,128]{2,1,0:T(8,128)(2,1)}, u32[]{:S(2)}) copy-start(bf16[42,128,128]{2,1,0:T(8,128)(2,1)} %get-tuple-element.4.local_in) | copy-start | bytes 4128772
  90.2 0.8 copy-start.1

commit v6 on v5

--- a/solution.py
+++ b/solution.py
@@ -88,9 +88,9 @@
     return (jnp.concatenate(solved, axis=0), own_separator)
 
 
-CHUNK = 2
+CHUNK = 3
 LINE = 4
-HOP = 2
+HOP = 1
 READY = HOP * (LINE - 1) + 1
 LEFT, RIGHT, ACROSS = 0, 1, 2
 MESH = pl.DeviceIdType.MESH
@@ -334,16 +334,8 @@
     for p in range(rows - 1):
         row_copy(2, p, slices[p], parts.at[row]).start()
 
-    def drain_rest(k, carry):
-        drain(k)
-        return carry
-
-    lax.fori_loop(chunks - 1, chunks, drain_rest, 0)
-    for p in range(rows - 1):
-        row_copy(0, p, top_rhs.at[row], top_rhs.at[row]).wait_send()
-        row_copy(1, p, held_top.at[row], held_top.at[row]).wait_send()
+    for p in range(rows - 1):
         row_arrival(1, p, held_top.at[peers[p]]).wait_recv()
-    pltpu.make_async_copy(sol, out_hbm, out_sem.at[0]).wait()
     for p in range(rows - 1):
         row_arrival(2, p, parts.at[peers[p]]).wait_recv()
 
@@ -381,34 +373,54 @@
     top_out[...] = owned.T.astype(jnp.bfloat16)
     last = pltpu.make_async_copy(top_out, top_out_hbm.at[0], out_sem.at[1])
     last.start()
-    for p in range(rows - 1):
+    def drain_rest(k, carry):
+        drain(k)
+        return carry
+
+    lax.fori_loop(chunks - 1, chunks, drain_rest, 0)
+    for p in range(rows - 1):
+        row_copy(0, p, top_rhs.at[row], top_rhs.at[row]).wait_send()
+        row_copy(1, p, held_top.at[row], held_top.at[row]).wait_send()
         row_copy(2, p, slices[p], parts.at[row]).wait_send()
     for t in range(rows):
         @pl.when(row != t)
         def _(t=t):
             solved_copy(t).wait_send()
+    pltpu.make_async_copy(sol, out_hbm, out_sem.at[0]).wait()
     last.wait()
 
 
-def place_kernel(local_in, top_in, local_out, top_out, sems):
-    copies = [
-        pltpu.make_async_copy(local_in, local_out, sems.at[0]),
-        pltpu.make_async_copy(top_in, top_out, sems.at[1]),
-    ]
-    for copy in copies:
-        copy.start()
-    for copy in copies:
-        copy.wait()
+def place_kernel(local_in, top_in, local_out, top_out, local_held, top_held, in_sem, out_sem):
+    pieces = len(range(0, local_in.shape[0], 2 * CHUNK))
+    size = local_in.shape[0] // pieces
+    parts = [pl.ds(index * size, size) for index in range(pieces)]
+    stages = [(local_in.at[part], local_held.at[part], local_out.at[part]) for part in parts]
+    stages.append((top_in, top_held, top_out))
+    fetches = [pltpu.make_async_copy(a, b, in_sem.at[index]) for index, (a, b, c) in enumerate(stages)]
+    stores = [pltpu.make_async_copy(b, c, out_sem.at[index]) for index, (a, b, c) in enumerate(stages)]
+    for fetch in fetches:
+        fetch.start()
+    for fetch, store in zip(fetches, stores):
+        fetch.wait()
+        store.start()
+    for store in stores:
+        store.wait()
 
 
 def placed(local_solution, top_solution):
+    pieces = len(range(0, local_solution.shape[0], 2 * CHUNK))
     return pl.pallas_call(
         place_kernel,
         out_shape=tuple(jax.ShapeDtypeStruct(x.shape, x.dtype) for x in (local_solution, top_solution)),
-        in_specs=[pl.BlockSpec(memory_space=pltpu.VMEM)] * 2,
+        in_specs=[pl.BlockSpec(memory_space=pl.ANY)] * 2,
         out_specs=(pl.BlockSpec(memory_space=pl.ANY),) * 2,
-        scratch_shapes=[pltpu.SemaphoreType.DMA((2,))],
-        compiler_params=pltpu.CompilerParams(vmem_limit_bytes=32 * 1024 * 1024),
+        scratch_shapes=[
+            pltpu.VMEM(local_solution.shape, local_solution.dtype),
+            pltpu.VMEM(top_solution.shape, top_solution.dtype),
+            pltpu.SemaphoreType.DMA((1 + pieces,)),
+            pltpu.SemaphoreType.DMA((1 + pieces,)),
+        ],
+        compiler_params=pltpu.CompilerParams(vmem_limit_bytes=60 * 1024 * 1024),
     )(local_solution, top_solution)
 
 

time: 92.3 us -> 89.4 us (0.969)
  local copies, waits for them, and re-layouts: 2.09 us -> 0 us
    unnamed x4 -> x0, local copies, waits for them, and re-layouts: 2.09 us -> none
    pallas_call x1, Pallas kernels: 88.2 us -> 86.3 us  [relayed(): pl.pallas_call(functools.partial(relay_kernel, rows), out_shape=(jax.Shap...]
    pallas_call x1, Pallas kernels: 1.1 us -> 2.23 us  [placed(): pl.pallas_call(place_kernel, out_shape=tuple((jax.ShapeDtypeStruct(x.shap...]
where the time goes in v6:
time: 89.4 us; the launch traced here: 89.2 us
  Pallas kernels  88.6 us (99%)
    pallas_call x1, Pallas kernels, relayed(): pl.pallas_call(functools.partial(relay_kernel, rows), out_shape=(jax.Shap...  86.3 us
    pallas_call x1, Pallas kernels, placed(): pl.pallas_call(place_kernel, out_shape=tuple((jax.ShapeDtypeStruct(x.shap...  2.23 us

profile of v6, /device:TPU:0, one launch (start us, length us, event | category | flops | bytes accessed | tf_op | source)
XLA Modules:
  0.0 89.2 jit_solution(7561689065630841512)
XLA Ops:
  0.6 86.3 %shard_map.86 = (bf16[42,128,128]{2,1,0:T(8,128)(2,1)}, bf16[1,128,128]{2,1,0:T(8,128)(2,1)}) custom-call(bf16[42,128,128]{2,1,0:T(8,128)(2,1)} %rhs_hbm.1, bf16[1,128,128]{2,1,0:T(8,128)(2,1)} %top_rhs_hbm.1, bf16[42,16,128]{2,1,0:T(8,128)(2,1)} %diag_hbm.1, bf16[1,16,128]{2,1,0:T(8,128)(2,1)} %top_inv_hbm.1, bf16[42,4,16,128]{3,2,1,0:T(8,128)(2,1)} %off_hbm.1, ...), custom_call_target="tpu_custom_call" | custom-call | flops 880803840 | bytes 3440640 | tf_op jit(solution)/shard_map/pallas_call | solution.py:433
  87.0 2.2 %shard_map.87 = (bf16[42,128,128]{2,1,0:T(8,128)(2,1)}, bf16[1,128,128]{2,1,0:T(8,128)(2,1)}) custom-call(bf16[42,128,128]{2,1,0:T(8,128)(2,1)} %get-tuple-element.4.local_in, bf16[1,128,128]{2,1,0:T(8,128)(2,1)} %get-tuple-element.5.top_in), custom_call_target="tpu_custom_call" | custom-call | tf_op jit(solution)/shard_map/pallas_call | solution.py:412

commit v7 on v6

--- a/solution.py
+++ b/solution.py
@@ -97,7 +97,7 @@
 
 
 def detour(k):
-    return lax.rem(k, 6) == 3
+    return (k > 0) & (lax.rem(k, 2) == 0)
 
 
 def times_turned(left, right):
@@ -181,44 +181,56 @@
     for p in range(rows - 1):
         row_copy(0, p, top_rhs.at[row], top_rhs.at[row]).start()
 
-    def either(k, src, count, act):
+    def straight_piece(k, src, count, act):
+        first = (k - 1) * CHUNK
+
         @pl.when(k == 0)
         def _():
             act(held_top.at[row, pl.ds(src, count)])
 
-        @pl.when(k > 0)
-        def _():
-            act(held.at[pl.ds(src, count), pl.ds((k - 1) * CHUNK, CHUNK)])
-
-    def describe(ref, k, src, way):
+        @pl.when((k > 0) & jnp.logical_not(detour(k)))
+        def _():
+            act(held.at[pl.ds(src, count), pl.ds(first, CHUNK)])
+
+        @pl.when(detour(k))
+        def _():
+            act(held.at[pl.ds(src, count), pl.ds(first, CHUNK - 1)])
+
+    def around_piece(k, src, count, act):
+        @pl.when(detour(k))
+        def _():
+            act(held.at[pl.ds(src, count), pl.ds(k * CHUNK - 1, 1)])
+
+    pieces = (straight_piece, around_piece)
+
+    def describe(ref, kind, k, src, way):
         return pltpu.make_async_remote_copy(
-            src_ref=ref, dst_ref=ref, send_sem=send_sem.at[way, k], recv_sem=recv_sem.at[k, src],
+            src_ref=ref, dst_ref=ref, send_sem=send_sem.at[kind, way, k], recv_sem=recv_sem.at[kind, k, src],
             device_id=(row, targets_of[way]), device_id_type=MESH,
         )
 
-    def relay(k, src, wait, ways):
+    def relay(kind, k, src, wait, ways):
         def act(ref):
             if wait:
-                describe(ref, k, src, ACROSS).wait_recv()
+                describe(ref, kind, k, src, ACROSS).wait_recv()
             for way, wanted in ways:
                 @pl.when(wanted)
                 def _(way=way):
-                    describe(ref, k, src, way).start()
-
-        either(k, src, 1, act)
+                    describe(ref, kind, k, src, way).start()
+
+        pieces[kind](k, src, 1, act)
 
     def drain(k):
-        around = detour(k)
-        sends = {
-            LEFT: jnp.where(z > 0, (LINE - z) * jnp.where(around, 2, 1), 0),
-            RIGHT: jnp.where(z < LINE - 1, (z + 1) * jnp.where(around, 2, 1), 0),
-            ACROSS: jnp.where(around, 1, LINE),
-        }
-        for way, sizes in ((LEFT, (1, 2, 3, 4, 6)), (RIGHT, (1, 2, 3, 4, 6)), (ACROSS, (1, LINE))):
-            for size in sizes:
-                @pl.when(sends[way] == size)
-                def _(way=way, size=size):
-                    either(k, 0, size, lambda ref: describe(ref, k, 0, way).wait_send())
+        left = jnp.where(z > 0, LINE - z, 0)
+        right = jnp.where(z < LINE - 1, z + 1, 0)
+        for kind in range(2):
+            for way, sends in ((LEFT, left), (RIGHT, right), (ACROSS, LINE)):
+                for count in (LINE,) if way == ACROSS else (1, 2, 3):
+                    size = (1 if way == ACROSS else 2 * count) if kind else count
+
+                    @pl.when(sends == count)
+                    def _(kind=kind, way=way, size=size):
+                        pieces[kind](k, 0, size, lambda ref: describe(ref, kind, k, 0, way).wait_send())
 
     def solve(k):
         first = (k - 1) * CHUNK
@@ -261,47 +273,47 @@
 
             @pl.when((k >= 0) & (k < chunks))
             def _(k=k, d=d):
-                straight = jnp.logical_not(detour(k))
                 if d == 0:
                     @pl.when(k == 2)
                     def _():
                         for copy in next_loads:
                             copy.wait()
 
-                    relay(k, me, False, ((LEFT, z > 0), (RIGHT, z < LINE - 1), (ACROSS, z >= 0)))
+                    for kind in range(2):
+                        relay(kind, k, me, False, ((LEFT, z > 0), (RIGHT, z < LINE - 1), (ACROSS, z >= 0)))
                 else:
                     @pl.when(z >= d)
                     def _():
-                        relay(k, me - 2 * d, True, ((RIGHT, z < LINE - 1), (ACROSS, straight)))
+                        relay(0, k, me - 2 * d, True, ((RIGHT, z < LINE - 1), (ACROSS, z >= 0)))
+                        relay(1, k, me - 2 * d, True, ((RIGHT, z < LINE - 1),))
 
                     @pl.when(z + d < LINE)
                     def _():
-                        relay(k, me + 2 * d, True, ((LEFT, z > 0), (ACROSS, straight)))
+                        relay(0, k, me + 2 * d, True, ((LEFT, z > 0), (ACROSS, z >= 0)))
+                        relay(1, k, me + 2 * d, True, ((LEFT, z > 0),))
 
             k = i - HOP * d - 1
 
-            @pl.when((k >= 0) & (k < chunks) & detour(k))
+            @pl.when((k >= 0) & (k < chunks))
             def _(k=k, d=d):
                 far = targets_of[ACROSS]
                 if d == 0:
-                    relay(k, far, True, ((LEFT, z > 0), (RIGHT, z < LINE - 1)))
+                    relay(1, k, far, True, ((LEFT, z > 0), (RIGHT, z < LINE - 1)))
                 else:
                     @pl.when(z >= d)
                     def _():
-                        relay(k, far - 2 * d, True, ((RIGHT, z < LINE - 1),))
+                        relay(1, k, far - 2 * d, True, ((RIGHT, z < LINE - 1),))
 
                     @pl.when(z + d < LINE)
                     def _():
-                        relay(k, far + 2 * d, True, ((LEFT, z > 0),))
+                        relay(1, k, far + 2 * d, True, ((LEFT, z > 0),))
 
         k = i - READY
 
         @pl.when(k >= 0)
         def _():
-            @pl.when(jnp.logical_not(detour(k)))
-            def _():
-                for other in range(LINE):
-                    relay(k, other * 2 + 1 - y, True, ())
+            for other in range(LINE):
+                relay(0, k, other * 2 + 1 - y, True, ())
 
             @pl.when(k == 0)
             def _():
@@ -455,8 +467,8 @@
             pltpu.VMEM((width, columns), bf16),
             pltpu.SemaphoreType.DMA((8,)),
             pltpu.SemaphoreType.DMA((2,)),
-            pltpu.SemaphoreType.DMA((3, chunks)),
-            pltpu.SemaphoreType.DMA((chunks, ranks)),
+            pltpu.SemaphoreType.DMA((2, 3, chunks)),
+            pltpu.SemaphoreType.DMA((2, chunks, ranks)),
             pltpu.SemaphoreType.DMA((3, rows - 1)),
             pltpu.SemaphoreType.DMA((3, rows)),
             pltpu.SemaphoreType.DMA((rows,)),

time: 89.4 us -> 90.1 us (level)
  no operation moved by 1% of the time
where the time goes in v7:
time: 90.1 us; the launch traced here: 90 us
  Pallas kernels  89.3 us (99%)
    pallas_call x1, Pallas kernels, relayed(): pl.pallas_call(functools.partial(relay_kernel, rows), out_shape=(jax.Shap...  87.1 us
    pallas_call x1, Pallas kernels, placed(): pl.pallas_call(place_kernel, out_shape=tuple((jax.ShapeDtypeStruct(x.shap...  2.23 us

profile of v7, /device:TPU:0, one launch (start us, length us, event | category | flops | bytes accessed | tf_op | source)
XLA Modules:
  0.0 90.0 jit_solution(10793982960516529558)
XLA Ops:
  0.6 87.1 %shard_map.86 = (bf16[42,128,128]{2,1,0:T(8,128)(2,1)}, bf16[1,128,128]{2,1,0:T(8,128)(2,1)}) custom-call(bf16[42,128,128]{2,1,0:T(8,128)(2,1)} %rhs_hbm.1, bf16[1,128,128]{2,1,0:T(8,128)(2,1)} %top_rhs_hbm.1, bf16[42,16,128]{2,1,0:T(8,128)(2,1)} %diag_hbm.1, bf16[1,16,128]{2,1,0:T(8,128)(2,1)} %top_inv_hbm.1, bf16[42,4,16,128]{3,2,1,0:T(8,128)(2,1)} %off_hbm.1, ...), custom_call_target="tpu_custom_call" | custom-call | flops 880803840 | bytes 3440640 | tf_op jit(solution)/shard_map/pallas_call | solution.py:445
  87.7 2.2 %shard_map.87 = (bf16[42,128,128]{2,1,0:T(8,128)(2,1)}, bf16[1,128,128]{2,1,0:T(8,128)(2,1)}) custom-call(bf16[42,128,128]{2,1,0:T(8,128)(2,1)} %get-tuple-element.4.local_in, bf16[1,128,128]{2,1,0:T(8,128)(2,1)} %get-tuple-element.5.top_in), custom_call_target="tpu_custom_call" | custom-call | tf_op jit(solution)/shard_map/pallas_call | solution.py:424

commit v8 on v6

--- a/solution.py
+++ b/solution.py
@@ -100,15 +100,11 @@
     return lax.rem(k, 6) == 3
 
 
-def times_turned(left, right):
-    return lax.dot_general(left, right, (((1,), (1,)), ((), ())), preferred_element_type=jnp.float32)
-
-
 def relay_kernel(
     rows, rhs_hbm, top_rhs_hbm, diag_hbm, top_inv_hbm, off_hbm, top_factor_hbm, targets,
     out_hbm, top_out_hbm,
     held, held_top, rhs, top_rhs, sol, acc, prod, part, parts, top_sol,
-    turned, top_rhs_turned, gathered, top_out,
+    turned, top_rhs_turned, gathered, top_out, top_turned,
     load_sem, out_sem, send_sem, recv_sem, row_send, row_recv, top_send, top_recv,
 ):
     sub, width, columns = rhs.shape
@@ -317,6 +313,18 @@
             def _():
                 solve(k)
 
+            @pl.when(k == 1)
+            def _():
+                for p in range(rows - 1):
+                    row_arrival(1, p, held_top.at[peers[p]]).wait_recv()
+
+            for t in range(rows):
+                @pl.when(k == t + 1)
+                def _(t=t):
+                    for block in range(t + 1):
+                        full = held_top[t, :, block].reshape(width, width).astype(jnp.float32)
+                        top_turned[t * 5 + block] = full.T.astype(jnp.bfloat16)
+
         @pl.when(i > READY)
         def _():
             drain(i - READY - 1)
@@ -335,8 +343,6 @@
         row_copy(2, p, slices[p], parts.at[row]).start()
 
     for p in range(rows - 1):
-        row_arrival(1, p, held_top.at[peers[p]]).wait_recv()
-    for p in range(rows - 1):
         row_arrival(2, p, parts.at[peers[p]]).wait_recv()
 
     def solved_copy(t):
@@ -345,17 +351,21 @@
             device_id=(t, me), device_id_type=MESH,
         )
 
+    bases = []
     for t in range(rows):
         base = turned[t, mine]
         for p in range(rows - 1):
             base = base + parts[peers[p], t].astype(jnp.float32)
-        base = top_rhs_turned[t, mine] - base
-        for earlier in range(t):
-            factor = held_top[t, :, 1 + earlier].reshape(width, width)
-            base = base - times_turned(top_sol[earlier], factor)
-        inverse = held_top[t, :, 0].reshape(width, width)
-        top_sol[t] = times_turned(base.astype(jnp.bfloat16), inverse).astype(jnp.bfloat16)
-
+        bases.append(top_rhs_turned[t, mine] - base)
+    for t in range(rows):
+        x = jnp.dot(bases[t].astype(jnp.bfloat16), top_turned[t * 5], preferred_element_type=jnp.float32)
+        x = x.astype(jnp.bfloat16)
+        top_sol[t] = x
+        for later in range(t + 1, rows):
+            bases[later] = bases[later] - jnp.dot(
+                x, top_turned[later * 5 + 1 + t], preferred_element_type=jnp.float32
+            )
+    for t in range(rows):
         @pl.when(row != t)
         def _(t=t):
             solved_copy(t).start()
@@ -453,6 +463,7 @@
             pltpu.VMEM((rows, columns, width), f32),
             pltpu.VMEM((rows, columns // rows, width), bf16),
             pltpu.VMEM((width, columns), bf16),
+            pltpu.VMEM((5 * rows, width, width), bf16),
             pltpu.SemaphoreType.DMA((8,)),
             pltpu.SemaphoreType.DMA((2,)),
             pltpu.SemaphoreType.DMA((3, chunks)),

time: 89.4 us -> 91.2 us (1.020)
  Pallas kernels: 88.6 us -> 90.4 us
    pallas_call x1, Pallas kernels: 86.3 us -> 88.2 us  [relayed(): pl.pallas_call(functools.partial(relay_kernel, rows), out_shape=(jax.Shap...]
where the time goes in v8:
time: 91.2 us; the launch traced here: 91.1 us
  Pallas kernels  90.4 us (99%)
    pallas_call x1, Pallas kernels, relayed(): pl.pallas_call(functools.partial(relay_kernel, rows), out_shape=(jax.Shap...  88.2 us
    pallas_call x1, Pallas kernels, placed(): pl.pallas_call(place_kernel, out_shape=tuple((jax.ShapeDtypeStruct(x.shap...  2.23 us

profile of v8, /device:TPU:0, one launch (start us, length us, event | category | flops | bytes accessed | tf_op | source)
XLA Modules:
  0.0 91.1 jit_solution(3740753240247985320)
XLA Ops:
  0.6 88.2 %shard_map.86 = (bf16[42,128,128]{2,1,0:T(8,128)(2,1)}, bf16[1,128,128]{2,1,0:T(8,128)(2,1)}) custom-call(bf16[42,128,128]{2,1,0:T(8,128)(2,1)} %rhs_hbm.1, bf16[1,128,128]{2,1,0:T(8,128)(2,1)} %top_rhs_hbm.1, bf16[42,16,128]{2,1,0:T(8,128)(2,1)} %diag_hbm.1, bf16[1,16,128]{2,1,0:T(8,128)(2,1)} %top_inv_hbm.1, bf16[42,4,16,128]{3,2,1,0:T(8,128)(2,1)} %off_hbm.1, ...), custom_call_target="tpu_custom_call" | custom-call | flops 880803840 | bytes 3440640 | tf_op jit(solution)/shard_map/pallas_call | solution.py:443
  88.8 2.2 %shard_map.87 = (bf16[42,128,128]{2,1,0:T(8,128)(2,1)}, bf16[1,128,128]{2,1,0:T(8,128)(2,1)}) custom-call(bf16[42,128,128]{2,1,0:T(8,128)(2,1)} %get-tuple-element.4.local_in, bf16[1,128,128]{2,1,0:T(8,128)(2,1)} %get-tuple-element.5.top_in), custom_call_target="tpu_custom_call" | custom-call | tf_op jit(solution)/shard_map/pallas_call | solution.py:422

commit v9 on v6

--- a/solution.py
+++ b/solution.py
@@ -97,7 +97,7 @@
 
 
 def detour(k):
-    return lax.rem(k, 6) == 3
+    return lax.rem(k, 6) == 4
 
 
 def times_turned(left, right):

time: 89.4 us -> 89.8 us (level)
  no operation moved by 1% of the time
where the time goes in v9:
time: 89.8 us; the launch traced here: 89.6 us
  Pallas kernels  89 us (99%)
    pallas_call x1, Pallas kernels, relayed(): pl.pallas_call(functools.partial(relay_kernel, rows), out_shape=(jax.Shap...  86.7 us
    pallas_call x1, Pallas kernels, placed(): pl.pallas_call(place_kernel, out_shape=tuple((jax.ShapeDtypeStruct(x.shap...  2.23 us

profile of v9, /device:TPU:0, one launch (start us, length us, event | category | flops | bytes accessed | tf_op | source)
XLA Modules:
  0.0 89.6 jit_solution(1699773313852899824)
XLA Ops:
  0.6 86.7 %shard_map.86 = (bf16[42,128,128]{2,1,0:T(8,128)(2,1)}, bf16[1,128,128]{2,1,0:T(8,128)(2,1)}) custom-call(bf16[42,128,128]{2,1,0:T(8,128)(2,1)} %rhs_hbm.1, bf16[1,128,128]{2,1,0:T(8,128)(2,1)} %top_rhs_hbm.1, bf16[42,16,128]{2,1,0:T(8,128)(2,1)} %diag_hbm.1, bf16[1,16,128]{2,1,0:T(8,128)(2,1)} %top_inv_hbm.1, bf16[42,4,16,128]{3,2,1,0:T(8,128)(2,1)} %off_hbm.1, ...), custom_call_target="tpu_custom_call" | custom-call | flops 880803840 | bytes 3440640 | tf_op jit(solution)/shard_map/pallas_call | solution.py:433
  87.4 2.2 %shard_map.87 = (bf16[42,128,128]{2,1,0:T(8,128)(2,1)}, bf16[1,128,128]{2,1,0:T(8,128)(2,1)}) custom-call(bf16[42,128,128]{2,1,0:T(8,128)(2,1)} %get-tuple-element.4.local_in, bf16[1,128,128]{2,1,0:T(8,128)(2,1)} %get-tuple-element.5.top_in), custom_call_target="tpu_custom_call" | custom-call | tf_op jit(solution)/shard_map/pallas_call | solution.py:412
